TPU v7x, 512 devices: a whole 4x4x16 slice. The times are simulated.
512 devices in a mesh: ctx: 32 (over z, core), head: 8 (over y, x_lo), dp: 2 (over x_hi).
Axes of the slice: x: 4 (x_hi: 2, x_lo: 2; x = x_hi * 2 + x_lo), y: 4, z: 16, core: 2. Of those that a mesh axis runs over, the one named last changes fastest.
Arguments:
- queries: bfloat16 [16384, 4096], P(('dp', 'ctx'), 'head'), parts along dimension 0, may hold values from -12 to 12
- keys_values: bfloat16 [2, 16384, 1024], P(None, ('dp', 'ctx'), 'head'), parts along dimension 1, may hold values from -12 to 12
- positions: int32 [16384], P(('dp', 'ctx')), parts along dimension 0, may hold values from 0 to 4096, as said below
- offsets: int32 [16], P('dp'), parts along dimension 0, may hold values from 0 to 8190, as said below
- w_out: bfloat16 [4096, 4096], P('head'), may hold values from -0.375 to 0.375
Outputs:
- mixed: bfloat16 [16384, 4096], P(('dp', 'ctx'), 'head'), parts along dimension 0
There are 2 independent parts, one for each index of `dp`. A program takes and returns all parts, laid end to end along the dimension named above; an argument that names none is the same for every part. Nothing has to cross between parts.
Inputs may be any that keep to these rules, and one draw needn't show every extreme that they name: offsets[0] = 0 and the offsets rise strictly; the first document holds exactly 4097 tokens and every later one two or more. positions[t] = t minus the largest offset not above t.
All inputs are finite; a program needn't handle non-finite values.
Results may differ from a plain program's by a relative error of at most 0.02.
Values may be sent and summed in bfloat16 or wider, within the bound.
A program may use at most 128 MiB of HBM per device.

v0:
```python
import math
import jax
import jax.numpy as jnp
from jax import lax
from jax.sharding import PartitionSpec as P

HD = 128
ROPE_BASE = 500000.0
STRETCH = 16.0
ANCHOR_LENGTH = 8192.0
BETA_FAST = 32.0
BETA_SLOW = 1.0
MAGNITUDE = 0.1 * math.log(16.0) + 1.0
NEGATIVE = -1e30


def tables(positions, width):
    half = width // 2
    index = jnp.arange(half, dtype=jnp.float32)
    base_freq = jnp.exp(index * (-2.0 * math.log(ROPE_BASE) / width))
    ratio = base_freq * (ANCHOR_LENGTH / (2.0 * math.pi))
    ramp = jnp.clip((ratio - BETA_SLOW) / (BETA_FAST - BETA_SLOW), 0.0, 1.0)
    freq = base_freq * (1.0 - ramp) / STRETCH + base_freq * ramp
    angle = positions.astype(jnp.float32)[:, None] * freq[None, :]
    return (jnp.cos(angle) * MAGNITUDE, jnp.sin(angle) * MAGNITUDE)


def rotate(field, cosine, sine):
    half = field.shape[-1] // 2
    first = field[..., :half]
    second = field[..., half:]
    cos_rows = cosine[:, None, :]
    sin_rows = sine[:, None, :]
    return jnp.concatenate(
        [first * cos_rows - second * sin_rows, second * cos_rows + first * sin_rows], axis=-1
    )


def shards(queries, keys_values, positions, offsets, w_out):
    rows = queries.shape[0]
    heads_here = w_out.shape[0] // HD
    cosine, sine = tables(positions, HD)
    rot_queries = (
        rotate(queries.reshape(rows, heads_here, HD).astype(jnp.float32), cosine, sine)
        * HD ** (-0.5)
    ).astype(jnp.bfloat16)
    rot_keys = (
        rotate(keys_values[0].reshape(rows, 1, HD).astype(jnp.float32), cosine, sine)
        .reshape(rows, HD)
        .astype(jnp.bfloat16)
    )
    moving = jnp.stack([rot_keys, keys_values[1]])
    first = lax.axis_index("ctx") * rows
    query_index = first + jnp.arange(rows, dtype=jnp.int32)
    starts = jnp.max(
        jnp.where(offsets[None, :] <= query_index[:, None], offsets[None, :], 0), axis=1
    )
    piece = lax.all_gather(moving, "ctx", axis=1, tiled=True)
    key_rows = piece[0]
    value_rows = piece[1]
    count = key_rows.shape[0]
    key_index = jnp.arange(count, dtype=jnp.int32)
    visible = (
        (key_index[None, :] <= query_index[:, None]) & (key_index[None, :] >= starts[:, None])
    )[:, None, :]
    scores = jnp.einsum("qhd,kd->qhk", rot_queries, key_rows, preferred_element_type=jnp.float32)
    peak = jnp.full((rows, heads_here), NEGATIVE, jnp.float32)
    new_peak = jnp.maximum(peak, jnp.max(jnp.where(visible, scores, NEGATIVE), axis=2))
    expo = jnp.where(visible, jnp.exp(scores - new_peak[..., None]), 0.0)
    total = jnp.sum(expo, axis=2)
    accum = jnp.einsum(
        "qhk,kd->qhd", expo.astype(jnp.bfloat16), value_rows, preferred_element_type=jnp.float32
    )
    result = (new_peak, total, accum)
    peak, total, accum = result
    attended = (accum / total[..., None]).astype(jnp.bfloat16).reshape(rows, heads_here * HD)
    partial_value = jnp.dot(attended, w_out, preferred_element_type=jnp.float32)
    return lax.psum_scatter(
        partial_value.astype(jnp.bfloat16), "head", scatter_dimension=1, tiled=True
    )


def solution(mesh):
    in_specs = (
        P(("dp", "ctx"), "head"),
        P(None, ("dp", "ctx"), "head"),
        P(("dp", "ctx")),
        P("dp"),
        P("head", None),
    )
    out_specs = P(("dp", "ctx"), "head")
    return jax.shard_map(shards, mesh=mesh, in_specs=in_specs, out_specs=out_specs, check_vma=False)
```

profile of v0, /device:TPU:1, one launch (start us, length us, event | category | flops | bytes accessed | tf_op | source)
XLA Modules:
  0.0 207.3 jit_solution(4234741551339588215)
XLA Ops:
  6.5 0.0 all-gather.2.cloned.1.call-start
  6.6 0.7 convert_element_type.48
  7.2 0.9 fusion.32
  8.1 0.1 copy.25
  8.3 0.1 copy.26
  8.4 0.3 fusion.22
  8.7 0.7 pad_maximum_fusion
  9.4 0.0 all-gather.2.cloned.1.call-update
  9.4 0.0 reduce-scatter.2.cloned.1.call-start
  9.5 1.1 copy.15
  10.6 0.2 copy.24
  10.8 0.2 copy.23
  11.0 0.7 select_reduce_fusion.1
  11.8 0.5 fusion.16
  12.3 0.1 multiply_subtract_fusion
  12.4 2.0 fusion.5
  14.4 80.9 %all-gather.2.cloned.1.call-done = bf16[2,8192,128]{1,2,0:T(8,128)(2,1)} async-done(((bf16[2,256,128]{1,2,0:T(8,128)(2,1)}), bf16[2,8192,128]{1,2,0:T(8,128)(2,1)}) %all-gather.2.cloned.1.call-update) | async-done | bytes 4194320 | tf_op jit(solution)/shard_map/all_gather | solution.py:58
  95.4 15.2 %select_reduce_fusion = (f32[256,4]{0,1:T(4,128)S(1)}, f32[256,4,8192]{2,0,1:T(8,128)}) fusion(pred[256,8192]{1,0:T(8,128)(4,1)S(1)} %fusion.5, bf16[2,8192,128]{1,2,0:T(8,128)(2,1)} %all-gather.2.cloned.1.call-done, f32[256,4,64]{2,0,1:T(8,128)S(1)} %get-tuple-element.6, f32[256,4,64]{2,0,1:T(8,128)S(1)} %get-tuple-element.5), kind=kOutput, calls=%fused_computation.1 | convolution fusion | flops 2164653056 | bytes 38277120 | tf_op jit(solution)/shard_map/qhd,kd->qhk/dot_general | solution.py:66
  110.5 14.7 %fusion = f32[256,4]{0,1:T(4,128)S(1)} fusion(f32[256,4,8192]{2,0,1:T(8,128)} %get-tuple-element.16, f32[256,4]{0,1:T(4,128)S(1)} %broadcast_maximum_fusion, pred[256,8192]{1,0:T(8,128)(4,1)S(1)} %fusion.5), kind=kLoop, calls=%fused_computation.2 | loop fusion | flops 25164800 | bytes 35659776 | tf_op jit(solution)/shard_map/reduce_sum | solution.py:70
  125.2 14.3 %fusion.10 = bf16[256,4,128]{0,2,1:T(8,128)(2,1)S(1)} fusion(bf16[2,8192,128]{1,2,0:T(8,128)(2,1)} %all-gather.2.cloned.1.call-done, f32[256,4,8192]{2,0,1:T(8,128)} %get-tuple-element.16, f32[256,4]{0,1:T(4,128)S(1)} %broadcast_maximum_fusion, pred[256,8192]{1,0:T(8,128)(4,1)S(1)} %fusion.5, f32[256,4]{0,1:T(4,128)S(1)} %fusion), kind=kOutput, calls=%fused_computation.14 | convolution fusion | flops 2172911616 | bytes 38019072 | tf_op jit(solution)/shard_map/qhk,kd->qhd/dot_general | solution.py:71
  139.5 4.8 %convolution_convert_fusion = bf16[256,4096]{1,0:T(8,128)(2,1)} fusion(bf16[256,512]{0,1:T(8,128)(2,1)S(1)} %bitcast.26, bf16[512,4096]{1,0:T(8,128)(2,1)} %param.9), kind=kOutput, calls=%fused_computation.9 | convolution fusion | flops 1074790400 | bytes 6553600 | tf_op jit(solution)/shard_map/dot_general | solution.py:77
  144.3 0.0 reduce-scatter.2.cloned.1.call-update
  144.3 56.2 %reduce-scatter.2.cloned.1.call-done = bf16[256,512]{1,0:T(8,128)(2,1)} async-done(((bf16[256,4096]{1,0:T(8,128)(2,1)}), bf16[256,512]{1,0:T(8,128)(2,1)}) %reduce-scatter.2.cloned.1.call-update) | async-done | bytes 262160 | tf_op jit(solution)/shard_map/reduce_scatter | solution.py:78
  (6 shorter events, 0.1 us)
Async XLA Ops:
  6.5 88.8 %all-gather.2.cloned.1.call-start = ((), (), s32[]{:S(2)}) async-start(), calls=%async_computation.1 | async-start | bytes 4325376 | tf_op jit(solution)/shard_map/all_gather | solution.py:58
  9.4 191.1 %reduce-scatter.2.cloned.1.call-start = ((), (), s32[]{:S(2)}) async-start(), calls=%async_computation.2 | async-start | bytes 2359296 | tf_op jit(solution)/shard_map/reduce_scatter | solution.py:78
Sparse Core Ops, SparseCore 0:
  9.5 85.7 all-gather.1
  144.4 56.0 reduce-scatter.1
where the time goes:
time: 208 us; the launch traced here: 207 us
  waiting for transfers between devices  137 us (66%)
  matrix products  34.2 us (16%)
  other arithmetic  19.8 us (10%)
  between operations  13.5 us (6%)
  local copies, waits for them, and re-layouts  2.61 us (1%)
    all_gather x1, waiting for transfers between devices, shards(): piece = lax.all_gather(moving, 'ctx', axis=1, tiled=True)  80.9 us
    reduce_scatter x1, waiting for transfers between devices, shards(): lax.psum_scatter(partial_value.astype(jnp.bfloat16), 'head', scatter_dime...  56.2 us
    dot_general x1, matrix products, shards(): jnp.einsum('qhd,kd->qhk', rot_queries, key_rows, preferred_element_type=j...  15.2 us
    reduce_sum x1, other arithmetic, shards(): total = jnp.sum(expo, axis=2)  14.7 us
    dot_general x1, matrix products, shards(): jnp.einsum('qhk,kd->qhd', expo.astype(jnp.bfloat16), value_rows, preferre...  14.3 us
    dot_general x1, matrix products, shards(): partial_value = jnp.dot(attended, w_out, preferred_element_type=jnp.float32)  4.81 us
  transfers between devices with their start and end apart: 2, of which 2 were waited for; matrix products, arithmetic and copies ran while one was open for 2% of the time, Pallas kernels for 0%

commit v1 on v0

--- a/solution.py
+++ b/solution.py
@@ -55,7 +55,9 @@
     starts = jnp.max(
         jnp.where(offsets[None, :] <= query_index[:, None], offsets[None, :], 0), axis=1
     )
-    piece = lax.all_gather(moving, "ctx", axis=1, tiled=True)
+    piece = jnp.concatenate(
+        lax.all_to_all(jnp.stack([moving] * lax.axis_size("ctx")), "ctx", 0, 0), axis=1
+    )
     key_rows = piece[0]
     value_rows = piece[1]
     count = key_rows.shape[0]

time: 208 us -> 330 us (1.59)
  waiting for transfers between devices: 137 us -> 239 us
  starting transfers between devices: 0.04 us -> 17 us
  local copies, waits for them, and re-layouts: 2.61 us -> 8.7 us
    all_to_all x0 -> x1, waiting for transfers between devices: none -> 180 us  [shards(): lax.all_to_all(jnp.stack([moving] * lax.axis_size('ctx')), 'ctx', 0, 0)]
    all_gather x1 -> x0, waiting for transfers between devices: 80.9 us -> none  [shards(): piece = lax.all_gather(moving, 'ctx', axis=1, tiled=True)]
    all_to_all x0 -> x1, starting transfers between devices: none -> 16.9 us  [shards(): lax.all_to_all(jnp.stack([moving] * lax.axis_size('ctx')), 'ctx', 0, 0)]
    slice x0 -> x1, local copies, waits for them, and re-layouts: none -> 3.92 us  [shards(): key_rows = piece[0]]
  transfers between devices with their start and end apart: 2 -> 2, of which waited for: 2 -> 2; matrix products, arithmetic and copies ran while one was open for 2% -> 1% of each run, Pallas kernels for 0% -> 0%
where the time goes in v1:
time: 330 us; the launch traced here: 329 us
  waiting for transfers between devices  239 us (72%)
  matrix products  32.7 us (10%)
  other arithmetic  18.4 us (6%)
  starting transfers between devices  17 us (5%)
  between operations  13.6 us (4%)
  local copies, waits for them, and re-layouts  8.7 us (3%)
    all_to_all x1, waiting for transfers between devices, shards(): lax.all_to_all(jnp.stack([moving] * lax.axis_size('ctx')), 'ctx', 0, 0)  180 us
    reduce_scatter x1, waiting for transfers between devices, shards(): lax.psum_scatter(partial_value.astype(jnp.bfloat16), 'head', scatter_dime...  59.1 us
    all_to_all x1, starting transfers between devices, shards(): lax.all_to_all(jnp.stack([moving] * lax.axis_size('ctx')), 'ctx', 0, 0)  16.9 us
    reduce_sum x1, other arithmetic, shards(): total = jnp.sum(expo, axis=2)  14.7 us
    dot_general x1, matrix products, shards(): jnp.einsum('qhk,kd->qhd', expo.astype(jnp.bfloat16), value_rows, preferre...  14.5 us
    dot_general x1, matrix products, shards(): jnp.einsum('qhd,kd->qhk', rot_queries, key_rows, preferred_element_type=j...  13.3 us
  transfers between devices with their start and end apart: 2, of which 2 were waited for; matrix products, arithmetic and copies ran while one was open for 1% of the time, Pallas kernels for 0%

profile of v1, /device:TPU:1, one launch (start us, length us, event | category | flops | bytes accessed | tf_op | source)
XLA Modules:
  0.0 329.3 jit_solution(3566332955605618457)
XLA Ops:
  6.6 0.7 convert_element_type.48
  7.2 0.9 fusion.33
  8.1 0.1 copy.29
  8.3 0.1 copy.30
  8.4 0.3 fusion.22
  8.7 0.1 copy.24
  8.9 3.0 stack.5
  11.9 0.0 copy-start
  11.9 0.0 copy-start.1
  11.9 16.9 %all-to-all-start = ((bf16[32,2,256,128]{3,2,1,0:T(8,128)(2,1)}), bf16[32,2,256,128]{3,2,1,0:T(8,128)(2,1)}, u32[]{:S(2)}, u32[]{:S(2)}) async-start(bf16[32,2,256,128]{3,2,1,0:T(8,128)(2,1)} %stack.5), calls=%async_computation | async-start | bytes 8388608 | tf_op jit(solution)/shard_map/all_to_all | solution.py:59
  28.8 0.0 reduce-scatter.2.cloned.1.call-start
  28.9 0.0 copy-done
  28.9 0.1 copy.19
  29.1 0.2 copy.28
  29.3 0.2 copy.27
  29.5 0.0 copy-done.1
  29.5 0.1 select_reduce_fusion.1
  29.6 0.5 fusion.16
  30.1 0.1 multiply_subtract_fusion
  30.2 2.0 fusion.5
  32.2 179.8 %all-to-all-done = bf16[32,2,256,128]{3,2,1,0:T(8,128)(2,1)} async-done(((bf16[32,2,256,128]{3,2,1,0:T(8,128)(2,1)}), bf16[32,2,256,128]{3,2,1,0:T(8,128)(2,1)}, u32[]{:S(2)}, u32[]{:S(2)}) %all-to-all-start) | async-done | bytes 4194336 | tf_op jit(solution)/shard_map/all_to_all | solution.py:59
  212.1 3.9 %fusion.31 = (bf16[1,32,256,128]{3,2,0,1:T(8,128)(2,1)S(1)}, bf16[1,32,256,128]{3,2,0,1:T(8,128)(2,1)}) fusion(bf16[2,32,256,128]{3,2,0,1:T(8,128)(2,1)} %bitcast.5), kind=kLoop, calls=%fused_computation.44 | loop fusion | bytes 8388608 | tf_op jit(solution)/shard_map/slice | solution.py:61
  216.0 13.3 %select_reduce_fusion = (f32[256,4]{0,1:T(4,128)S(1)}, f32[256,4,8192]{2,0,1:T(8,128)}) fusion(pred[256,8192]{1,0:T(8,128)(4,1)S(1)} %fusion.5, bf16[8192,128,1]{1,0,2:T(8,128)(2,1)S(1)} %bitcast.20, f32[256,4,64]{2,0,1:T(8,128)S(1)} %get-tuple-element.8, f32[256,4,64]{2,0,1:T(8,128)S(1)} %get-tuple-element.7), kind=kOutput, calls=%fused_computation.1 | convolution fusion | flops 2164653056 | bytes 38277120 | tf_op jit(solution)/shard_map/qhd,kd->qhk/dot_general | solution.py:68
  229.3 14.7 %fusion = f32[256,4]{0,1:T(4,128)S(1)} fusion(f32[256,4,8192]{2,0,1:T(8,128)} %get-tuple-element.18, f32[256,4]{0,1:T(4,128)S(1)} %broadcast_maximum_fusion, pred[256,8192]{1,0:T(8,128)(4,1)S(1)} %fusion.5), kind=kLoop, calls=%fused_computation.2 | loop fusion | flops 25164800 | bytes 35659776 | tf_op jit(solution)/shard_map/reduce_sum | solution.py:72
  244.0 14.5 %fusion.9 = bf16[256,4,128]{0,2,1:T(8,128)(2,1)S(1)} fusion(bf16[8192,128,1]{1,0,2:T(8,128)(2,1)} %bitcast.22, f32[256,4,8192]{2,0,1:T(8,128)} %get-tuple-element.18, f32[256,4]{0,1:T(4,128)S(1)} %broadcast_maximum_fusion, pred[256,8192]{1,0:T(8,128)(4,1)S(1)} %fusion.5, f32[256,4]{0,1:T(4,128)S(1)} %fusion), kind=kOutput, calls=%fused_computation.11 | convolution fusion | flops 2172911616 | bytes 38019072 | tf_op jit(solution)/shard_map/qhk,kd->qhd/dot_general | solution.py:73
  258.5 4.8 %convolution_convert_fusion = bf16[256,4096]{1,0:T(8,128)(2,1)} fusion(bf16[256,512]{0,1:T(8,128)(2,1)S(1)} %bitcast.23, bf16[512,4096]{1,0:T(8,128)(2,1)} %param.9), kind=kOutput, calls=%fused_computation.9 | convolution fusion | flops 1074790400 | bytes 6553600 | tf_op jit(solution)/shard_map/dot_general | solution.py:79
  263.3 0.0 reduce-scatter.2.cloned.1.call-update
  263.4 59.1 %reduce-scatter.2.cloned.1.call-done = bf16[256,512]{1,0:T(8,128)(2,1)} async-done(((bf16[256,4096]{1,0:T(8,128)(2,1)}), bf16[256,512]{1,0:T(8,128)(2,1)}) %reduce-scatter.2.cloned.1.call-update) | async-done | bytes 262160 | tf_op jit(solution)/shard_map/reduce_scatter | solution.py:80
  (7 shorter events, 0.1 us)
Async XLA Ops:
  11.9 17.0 %copy-start = (bf16[256,512]{1,0:T(8,128)(2,1)S(1)}, bf16[256,512]{1,0:T(8,128)(2,1)}, u32[]{:S(2)}) copy-start(bf16[256,512]{1,0:T(8,128)(2,1)} %param.5) | copy-start | bytes 786436
  11.9 17.6 %copy-start.1 = (s32[8]{0:T(128)S(1)}, s32[8]{0:T(128)}, u32[]{:S(2)}) copy-start(s32[8]{0:T(128)} %param.8) | copy-start | bytes 100
  11.9 200.2 %all-to-all-start = ((bf16[32,2,256,128]{3,2,1,0:T(8,128)(2,1)}), bf16[32,2,256,128]{3,2,1,0:T(8,128)(2,1)}, u32[]{:S(2)}, u32[]{:S(2)}) async-start(bf16[32,2,256,128]{3,2,1,0:T(8,128)(2,1)} %stack.5), calls=%async_computation | async-start | bytes 8388608 | tf_op jit(solution)/shard_map/all_to_all | solution.py:59
  28.8 293.6 %reduce-scatter.2.cloned.1.call-start = ((), (), s32[]{:S(2)}) async-start(), calls=%async_computation.2 | async-start | bytes 2359296 | tf_op jit(solution)/shard_map/reduce_scatter | solution.py:80
Sparse Core Ops, SparseCore 0:
  263.5 58.8 reduce-scatter.1
